TPU v7x, 32 devices: a whole 2x2x4 slice. The times are simulated.
32 devices in a mesh: pool: 2 (over core), pb: 4 (over z), ka: 4 (over y, x).
Axes of the slice: x: 2, y: 2, z: 4, core: 2. Of those that a mesh axis runs over, the one named last changes fastest.
Arguments:
- tokens: bfloat16 [2048, 5376], P(('pb', 'ka'), 'pool'), may hold values from -6 to 6
- modality: int32 [2048], P('pb'), may hold values from 0 to 1, as said below
- proj_weight: bfloat16 [2, 5376, 2048], P('pool', None, 'ka'), may hold values from -0.078125 to 0.078125
- out_grad: bfloat16 [2, 2048, 512], P('pool', 'pb', 'ka'), may hold values from -24 to 24
Outputs:
- grad_tokens: bfloat16 [2048, 5376], P(('pb', 'ka'), 'pool')
- grad_weight: float32 [2, 5376, 2048], P('pool', 'pb', 'ka')
Inputs may be any that keep to these rules, and one draw needn't show every extreme that they name: `modality`: 1 marks image tokens; they stand in runs whose lengths are multiples of 256 except at the sequence's start and end, and both kinds occur.
All inputs are finite; a program needn't handle non-finite values.
Results may differ from a plain program's by a relative error of at most 0.018.
Values may be sent and summed in bfloat16 or wider, within the bound.
A program may use at most 192 MiB of HBM per device.

v0:
```python
import math

import jax
import jax.numpy as jnp
from jax import lax
from jax.sharding import PartitionSpec as P


def shards(tokens, modality, proj_weight, out_grad):
    contract_one = (((1,), (1,)), ((), ()))
    contract_zero = (((0,), (0,)), ((), ()))
    pool_index = lax.axis_index("pool")
    pool_count = lax.axis_size("pool")
    head_size = out_grad.shape[2]
    scaling = 1.0 / math.sqrt(head_size)
    token_count = tokens.shape[0]
    half_width = tokens.shape[1]
    group_width = proj_weight.shape[2]
    weight = proj_weight[0].reshape(pool_count, half_width, group_width)
    gathered = lax.all_gather(tokens[None], ("pool", "ka"), axis=0, tiled=True)
    query_count = gathered.shape[0] // pool_count * token_count
    block_tokens = gathered.reshape(pool_count, query_count, half_width)
    owned = (modality == pool_index)[:, None]
    local_proj = jnp.where(
        owned,
        lax.dot_general(
            block_tokens, weight, (((0, 2), (0, 1)), ((), ())), preferred_element_type=jnp.float32
        ),
        0.0,
    )
    projected = lax.psum(local_proj.astype(jnp.bfloat16), "pool")
    queries = lax.dynamic_slice_in_dim(projected, pool_index * head_size, head_size, 1)
    half_rows = query_count // pool_count
    own_keys = projected[:, group_width - 2 * head_size :].reshape(
        pool_count, half_rows, 2 * head_size
    )
    key_value = lax.all_gather(own_keys, "pb", axis=1, tiled=True).reshape(-1, 2 * head_size)
    key_rows = key_value[:, :head_size]
    value_rows = key_value[:, head_size:]
    cotangent = out_grad[0]
    tile_rows = min(512, query_count)
    tile_count = query_count // tile_rows
    q_tiles = queries.reshape(tile_count, tile_rows, head_size)
    o_tiles = cotangent.reshape(tile_count, tile_rows, head_size)

    def advance(running, tile_in):
        q_tile, o_tile = tile_in
        scores = (
            lax.dot_general(q_tile, key_rows, contract_one, preferred_element_type=jnp.float32)
            * scaling
        )
        row_max = jnp.max(scores, axis=1, keepdims=True)
        log_total = row_max + jnp.log(jnp.sum(jnp.exp(scores - row_max), axis=1, keepdims=True))
        softmax = jnp.exp(scores - log_total)
        grad_prob = lax.dot_general(
            o_tile, value_rows, contract_one, preferred_element_type=jnp.float32
        )
        delta = jnp.sum(softmax * grad_prob, axis=1, keepdims=True)
        grad_score = (softmax * (grad_prob - delta)).astype(jnp.bfloat16)
        grad_query = jnp.dot(grad_score, key_rows, preferred_element_type=jnp.float32) * scaling
        new_keys = (
            running[0]
            + lax.dot_general(grad_score, q_tile, contract_zero, preferred_element_type=jnp.float32)
            * scaling
        )
        new_values = running[1] + lax.dot_general(
            softmax.astype(jnp.bfloat16), o_tile, contract_zero, preferred_element_type=jnp.float32
        )
        return ((new_keys, new_values), grad_query)

    key_count = key_rows.shape[0]
    start_state = (
        jnp.zeros((key_count, head_size), jnp.float32),
        jnp.zeros((key_count, head_size), jnp.float32),
    )
    (grad_keys, grad_values), grad_query = lax.scan(advance, start_state, (q_tiles, o_tiles))
    key_terms = jnp.concatenate([grad_keys, grad_values], axis=1)
    key_cell = lax.psum_scatter(
        key_terms.astype(jnp.bfloat16), ("pool", "pb"), scatter_dimension=0, tiled=True
    )
    query_low = grad_query.reshape(query_count, head_size).astype(jnp.bfloat16)
    both_queries, key_block = (
        lax.all_gather(query_low, "pool", axis=1, tiled=True),
        lax.all_gather(key_cell, "pool", axis=0, tiled=True),
    )
    grad_proj = jnp.concatenate([both_queries, key_block], axis=1)
    masked = jnp.where(owned, grad_proj, jnp.zeros_like(grad_proj))
    back = jnp.einsum("rj,pcj->prc", masked, weight, preferred_element_type=jnp.float32)
    stacked = back.reshape(pool_count * (query_count // token_count), token_count, half_width)
    token_sum = lax.psum_scatter(
        stacked.astype(jnp.bfloat16), ("pool", "ka"), scatter_dimension=0, tiled=True
    ).astype(jnp.float32)[0]
    grad_tokens = token_sum.astype(jnp.bfloat16)
    term = jnp.einsum(
        "prc,rj->pcj", block_tokens, masked, preferred_element_type=jnp.float32
    ).reshape(-1, group_width)
    grad_weight = lax.psum_scatter(
        term.astype(jnp.bfloat16), "pb", scatter_dimension=0, tiled=True
    ).astype(jnp.float32)
    return (grad_tokens, grad_weight[None])


def solution(mesh):
    return jax.shard_map(
        shards,
        mesh=mesh,
        in_specs=(P(("pb", "ka"), "pool"), P("pb"), P("pool", None, "ka"), P("pool", "pb", "ka")),
        out_specs=(P(("pb", "ka"), "pool"), P("pool", "pb", "ka")),
        check_vma=False,
    )
```

profile of v0, /device:TPU:10, one launch (start us, length us, event | category | flops | bytes accessed | tf_op | source)
XLA Modules:
  0.0 340.6 jit_solution(5645796647985201788)
XLA Ops:
  7.2 0.7 all-gather.6.cloned.1.call-update
  8.0 0.7 broadcast_compare_fusion
  8.7 44.6 %all-gather.6.cloned.1.call-done = bf16[1024,2688]{1,0:T(8,128)(2,1)} async-done(((bf16[128,2688]{1,0:T(8,128)(2,1)}), bf16[1024,2688]{1,0:T(8,128)(2,1)}) %all-gather.6.cloned.1.call-update) | async-done | bytes 5505040 | tf_op jit(solution)/shard_map/all_gather | solution.py:20
  53.3 8.0 %fusion.10 = bf16[512,512]{1,0:T(8,128)(2,1)} fusion(bf16[2,512,2688]{2,1,0:T(8,128)(2,1)} %bitcast.55, bf16[2,2688,512]{2,1,0:T(8,128)(2,1)} %bitcast.53, pred[512]{0:T(512)(128)(4,1)S(1)} %broadcast_compare_fusion), kind=kOutput, calls=%fused_computation.20 | convolution fusion | flops 2819096576 | bytes 11534848 | tf_op jit(solution)/shard_map/dot_general | solution.py:26
  61.3 19.1 %all-reduce.2.cloned.1.call-done = bf16[512,512]{1,0:T(8,128)(2,1)} async-done(((bf16[512,512]{1,0:T(8,128)(2,1)}), bf16[512,512]{1,0:T(8,128)(2,1)}) %all-reduce.2.cloned.1.call-update) | async-done | bytes 524304 | tf_op jit(solution)/shard_map/psum | solution.py:31
  80.5 1.7 slice.12
  82.2 29.3 %all-gather.4.cloned.1.call-done = bf16[2,1024,256]{2,1,0:T(8,128)(2,1)} async-done(((bf16[2,256,256]{2,1,0:T(8,128)(2,1)}), bf16[2,1024,256]{2,1,0:T(8,128)(2,1)}) %all-gather.4.cloned.1.call-update) | async-done | bytes 1048592 | tf_op jit(solution)/shard_map/all_gather | solution.py:37
  111.5 2.0 multiply_reduce_fusion
  113.5 0.8 exponential_reduce_fusion
  114.4 1.2 fusion.1
  115.5 1.2 convolution_convert_fusion.2
  116.8 1.0 fusion.3
  117.8 1.7 fusion.5
  119.5 1.1 pad_maximum_fusion
  120.6 0.7 fusion.11
  121.3 2.0 all_gather.14
  123.3 30.3 %reduce-scatter.4.cloned.1.call-done = bf16[256,256]{1,0:T(8,128)(2,1)} async-done(((bf16[2048,256]{1,0:T(8,128)(2,1)}), bf16[256,256]{1,0:T(8,128)(2,1)}) %reduce-scatter.4.cloned.1.call-update) | async-done | bytes 131088 | tf_op jit(solution)/shard_map/reduce_scatter | solution.py:78
  153.7 2.2 all_gather.15
  155.8 7.6 %fusion = bf16[2,2688,512]{1,2,0:T(8,128)(2,1)} fusion(bf16[2,512,2688]{2,1,0:T(8,128)(2,1)} %bitcast.56, bf16[512,256]{1,0:T(8,128)(2,1)S(1)} %all_gather.15, bf16[512,256]{1,0:T(8,128)(2,1)S(1)} %all_gather.14, pred[512]{0:T(512)(128)(4,1)S(1)} %broadcast_compare_fusion), kind=kOutput, calls=%fused_computation.2 | convolution fusion | flops 2822635520 | bytes 11534848 | tf_op jit(solution)/shard_map/prc,rj->pcj/dot_general | solution.py:94
  163.4 8.3 %copy.14 = bf16[2,2688,512]{2,1,0:T(8,128)(2,1)} copy(bf16[2,2688,512]{1,2,0:T(8,128)(2,1)} %fusion) | data formatting | bytes 11010048 | tf_op jit(solution)/shard_map/convert_element_type | solution.py:98
  171.8 7.5 %convolution_convert_fusion.1 = bf16[512,2,2688]{2,0,1:T(8,128)(2,1)} fusion(bf16[2,2688,512]{2,1,0:T(8,128)(2,1)} %bitcast.54, bf16[512,256]{1,0:T(8,128)(2,1)S(1)} %all_gather.15, bf16[512,256]{1,0:T(8,128)(2,1)S(1)} %all_gather.14, pred[512]{0:T(512)(128)(4,1)S(1)} %broadcast_compare_fusion), kind=kOutput, calls=%fused_computation.1 | convolution fusion | flops 2822635520 | bytes 11534848 | tf_op jit(solution)/shard_map/rj,pcj->prc/dot_general | solution.py:88
  179.3 91.8 %reduce-scatter.8.cloned.1.call-done = bf16[1344,512]{1,0:T(8,128)(2,1)} async-done(((bf16[5376,512]{1,0:T(8,128)(2,1)}), bf16[1344,512]{1,0:T(8,128)(2,1)}) %reduce-scatter.8.cloned.1.call-update) | async-done | bytes 1376272 | tf_op jit(solution)/shard_map/reduce_scatter | solution.py:97
  271.1 3.3 bitcast_convert_fusion
  274.4 59.3 %reduce-scatter.6.cloned.1.call-done = bf16[1,128,2688]{2,1,0:T(8,128)(2,1)} async-done(((bf16[8,128,2688]{2,1,0:T(8,128)(2,1)}), bf16[1,128,2688]{2,1,0:T(8,128)(2,1)}) %reduce-scatter.6.cloned.1.call-update) | async-done | bytes 688144 | tf_op jit(solution)/shard_map/reduce_scatter | solution.py:90
  (16 shorter events, 0.3 us)
Async XLA Ops:
  7.2 107.2 %copy-start = (bf16[1,512,128]{2,1,0:T(8,128)(2,1)S(1)}, bf16[1,512,128]{2,1,0:T(8,128)(2,1)}, u32[]{:S(2)}) copy-start(bf16[1,512,128]{2,1,0:T(8,128)(2,1)} %param.7) | copy-start | bytes 393220
  7.2 46.1 %all-gather.6.cloned.1.call-start = ((), (), s32[]{:S(2)}) async-start(), calls=%async_computation.8 | async-start | bytes 6193152 | tf_op jit(solution)/shard_map/all_gather | solution.py:20
  7.9 72.5 %all-reduce.2.cloned.1.call-start = ((), (), s32[]{:S(2)}) async-start(), calls=%async_computation.3 | async-start | bytes 1048576 | tf_op jit(solution)/shard_map/psum | solution.py:31
  61.3 50.2 %all-gather.4.cloned.1.call-start = ((), (), s32[]{:S(2)}) async-start(), calls=%async_computation.4 | async-start | bytes 1310720 | tf_op jit(solution)/shard_map/all_gather | solution.py:37
  82.2 71.5 %reduce-scatter.4.cloned.1.call-start = ((), (), s32[]{:S(2)}) async-start(), calls=%async_computation.5 | async-start | bytes 1179648 | tf_op jit(solution)/shard_map/reduce_scatter | solution.py:78
  111.5 2.8 copy-start.1
  120.6 150.6 %reduce-scatter.8.cloned.1.call-start = ((), (), s32[]{:S(2)}) async-start(), calls=%async_computation.7 | async-start | bytes 6881280 | tf_op jit(solution)/shard_map/reduce_scatter | solution.py:97
  171.7 162.0 %reduce-scatter.6.cloned.1.call-start = ((), (), s32[]{:S(2)}) async-start(), calls=%async_computation.6 | async-start | bytes 6193152 | tf_op jit(solution)/shard_map/reduce_scatter | solution.py:90
Sparse Core Ops, SparseCore 0:
  9.9 43.3 all-gather.5
  61.4 18.9 all-reduce.1
  82.7 28.7 all-gather.3
  120.7 32.9 reduce-scatter.3
  171.8 99.2 reduce-scatter.7
  275.4 58.2 reduce-scatter.5
where the time goes:
time: 343 us; the launch traced here: 341 us
  waiting for transfers between devices  275 us (80%)
  matrix products  29.8 us (9%)
  between operations  14.2 us (4%)
  local copies, waits for them, and re-layouts  9.96 us (3%)
  other arithmetic  6.9 us (2%)
  blocking collectives  4.19 us (1%)
    reduce_scatter x1, waiting for transfers between devices, shards(): lax.psum_scatter(term.astype(jnp.bfloat16), 'pb', scatter_dimension=0, ti...  91.8 us
    reduce_scatter x1, waiting for transfers between devices, shards(): lax.psum_scatter(stacked.astype(jnp.bfloat16), ('pool', 'ka'), scatter_di...  59.3 us
    all_gather x1, waiting for transfers between devices, shards(): gathered = lax.all_gather(tokens[None], ('pool', 'ka'), axis=0, tiled=True)  44.6 us
    reduce_scatter x1, waiting for transfers between devices, shards(): lax.psum_scatter(key_terms.astype(jnp.bfloat16), ('pool', 'pb'), scatter_...  30.3 us
    all_gather x1, waiting for transfers between devices, shards(): lax.all_gather(own_keys, 'pb', axis=1, tiled=True)  29.3 us
    psum x1, waiting for transfers between devices, shards(): projected = lax.psum(local_proj.astype(jnp.bfloat16), 'pool')  19.1 us
    convert_element_type x1, local copies, waits for them, and re-layouts, shards(): term.astype(jnp.bfloat16)  8.28 us
    dot_general x1, matrix products, shards(): lax.dot_general(block_tokens, weight, (((0, 2), (0, 1)), ((), ())), prefe...  7.99 us
  transfers between devices with their start and end apart: 6, of which 6 were waited for; matrix products, arithmetic and copies ran while one was open for 4% of the time, Pallas kernels for 0%

commit v1 on v0

--- a/solution.py
+++ b/solution.py
@@ -1,12 +1,15 @@
+import functools
 import math
 
 import jax
 import jax.numpy as jnp
 from jax import lax
+from jax.experimental import pallas as pl
+from jax.experimental.pallas import tpu as pltpu
 from jax.sharding import PartitionSpec as P
 
 
-def shards(tokens, modality, proj_weight, out_grad):
+def plain_shards(tokens, modality, proj_weight, out_grad):
     contract_one = (((1,), (1,)), ((), ()))
     contract_zero = (((0,), (0,)), ((), ()))
     pool_index = lax.axis_index("pool")
@@ -100,6 +103,362 @@
     return (grad_tokens, grad_weight[None])
 
 
+BF16 = jnp.bfloat16
+F32 = jnp.float32
+NT = (((1,), (1,)), ((), ()))
+
+
+def divisor(total, unit, most):
+    best = unit
+    for size in range(unit, most + 1, unit):
+        if total % size == 0:
+            best = size
+    return best
+
+
+def fused(
+    dims, tok, xt, mod, weight_hbm, cot, out_tok, out_weight,
+    tokbuf, wbuf, xtbuf, modbuf, projloc, projrecv, qbuf, kvbuf, ktbuf, dkacc, dvacc,
+    dkv, dkvp, dkvs, dkvr, gp, mgp, bsend, brecv, bsum, kar, load_sem, ss, rs,
+):
+    n_pb, n_ka, rows, half, group, hd, q_rows, offsets = dims
+    scaling = 1.0 / math.sqrt(hd)
+    p, b, k = lax.axis_index("pool"), lax.axis_index("pb"), lax.axis_index("ka")
+    other = 1 - p
+    q_half = q_rows // 2
+    hp = n_pb // 2
+    n_c, chunk = bsend.shape[0], bsend.shape[2]
+    slice_rows = xt.shape[1]
+    kv_at = group - 2 * hd
+    partner = (other, b, k)
+    sends = []
+
+    def pb_dev(d):
+        return (p, lax.rem(b + d, n_pb), k)
+
+    def ka_dev(d):
+        return (p, b, lax.rem(k + d, n_ka))
+
+    def b_from(d):
+        return lax.rem(b - d + n_pb, n_pb)
+
+    def k_from(d):
+        return lax.rem(k - d + n_ka, n_ka)
+
+    def remote(src, dst, name, i, dev):
+        at = offsets[name] + i
+        return pltpu.make_async_remote_copy(
+            src_ref=src, dst_ref=dst, send_sem=ss.at[at], recv_sem=rs.at[at],
+            device_id=dev, device_id_type=pl.DeviceIdType.MESH,
+        )
+
+    def send(src, dst, name, i, dev):
+        copy = remote(src, dst, name, i, dev)
+        copy.start()
+        sends.append(copy)
+
+    def arrived(dst, name, i):
+        remote(dst, dst, name, i, partner).wait_recv()
+
+    def ka_rows(index):
+        return pl.ds(pl.multiple_of(index * rows, rows), rows)
+
+    barrier = pltpu.get_barrier_semaphore()
+    devs = [partner] + [pb_dev(d) for d in range(1, n_pb)] + [ka_dev(d) for d in range(1, n_ka)]
+    for dev in devs:
+        pl.semaphore_signal(barrier, inc=1, device_id=dev, device_id_type=pl.DeviceIdType.MESH)
+    load = pltpu.make_async_copy(weight_hbm.at[0], wbuf, load_sem)
+    load.start()
+    pl.semaphore_wait(barrier, len(devs))
+
+    for d in range(1, n_ka):
+        send(tok, tokbuf.at[p, ka_rows(k)], "tok_ka", d, ka_dev(d))
+    send(tok, tokbuf.at[p, ka_rows(k)], "tok_fw", 0, partner)
+    for d in range(1, n_pb):
+        send(mod, modbuf.at[b], "mod", d, pb_dev(d))
+
+    mine = lax.div(b, hp) == p
+    for d in range(1, n_pb):
+        target = lax.rem(b + d, n_pb)
+
+        @pl.when(lax.div(target, hp) == p)
+        def _(d=d, target=target):
+            remote(
+                xt.at[lax.rem(target, hp)], xtbuf.at[b, :, ka_rows(k)], "xt_z", d, pb_dev(d)
+            ).start()
+
+    tokbuf[p, ka_rows(k), :] = tok[...]
+    modbuf[b] = mod[...]
+
+    @pl.when(mine)
+    def _():
+        xtbuf[b, :, ka_rows(k)] = xt[lax.rem(b, hp)]
+
+    for d in range(1, n_ka):
+        region = tokbuf.at[p, ka_rows(k_from(d))]
+        arrived(region, "tok_ka", d)
+        send(region, region, "tok_fw", d, partner)
+    for d in range(n_ka):
+        arrived(tokbuf.at[other, ka_rows(k_from(d))], "tok_fw", d)
+    load.wait()
+
+    def own_mask(index):
+        return modbuf[index].astype(F32)[:, :1] == p.astype(F32)
+
+    proj = jnp.dot(tokbuf[0], wbuf[:half], preferred_element_type=F32)
+    proj += jnp.dot(tokbuf[1], wbuf[half:], preferred_element_type=F32)
+    projloc[...] = proj.astype(BF16)
+    send(projloc, projrecv, "pj", 0, partner)
+
+    @pl.when(mine)
+    def _():
+        for d in range(1, n_pb):
+            arrived(xtbuf.at[b_from(d), :, ka_rows(k)], "xt_z", d)
+        for d in range(1, n_ka):
+            region = xtbuf.at[:, :, ka_rows(k)]
+            remote(region, region, "xt_ka", d, ka_dev(d)).start()
+        region = xtbuf.at[:, :, ka_rows(k)]
+        remote(region, region, "xt_fw", 0, partner).start()
+
+    arrived(projrecv, "pj", 0)
+    projected = jnp.where(own_mask(b), projloc[...].astype(F32), projrecv[...].astype(F32)).astype(BF16)
+    qbuf[...] = jnp.where(p == 0, projected[:, :hd].astype(F32), projected[:, hd : 2 * hd].astype(F32)).astype(BF16)
+    kvbuf[b] = projected[:, kv_at:].reshape(2, q_half, 2 * hd)
+    for d in range(1, n_pb):
+        send(kvbuf.at[b, p], kvbuf.at[b, p], "kv_z", d, pb_dev(d))
+    for d in range(1, n_pb):
+        region = kvbuf.at[b_from(d), p]
+        arrived(region, "kv_z", d)
+        send(region, region, "kv_fw", d, partner)
+    for d in range(1, n_pb):
+        arrived(kvbuf.at[b_from(d), other], "kv_fw", d)
+
+    keys = n_pb * q_rows
+    ktbuf[...] = jnp.transpose(
+        kvbuf[:, :, :, :hd].reshape(keys, hd).astype(F32)
+    ).astype(BF16)
+    dkacc[...] = jnp.zeros_like(dkacc)
+    dvacc[...] = jnp.zeros_like(dvacc)
+    tile = min(256, q_rows)
+
+    def attend(t, carry):
+        at = pl.ds(pl.multiple_of(t * tile, tile), tile)
+        q = qbuf[at, :]
+        o = cot[0, at, :]
+        key_rows = kvbuf[:, :, :, :hd].reshape(keys, hd)
+        value_rows = kvbuf[:, :, :, hd:].reshape(keys, hd)
+        scores = lax.dot_general(key_rows, q, NT, preferred_element_type=F32) * scaling
+        high = jnp.max(scores, axis=0, keepdims=True)
+        raised = jnp.exp(scores - high)
+        softmax = raised * (1.0 / jnp.sum(raised, axis=0, keepdims=True))
+        grad_prob = lax.dot_general(value_rows, o, NT, preferred_element_type=F32)
+        delta = jnp.sum(softmax * grad_prob, axis=0, keepdims=True)
+        grad_score = (softmax * (grad_prob - delta)).astype(BF16)
+        dkacc[...] += jnp.dot(grad_score, q, preferred_element_type=F32)
+        dvacc[...] += jnp.dot(softmax.astype(BF16), o, preferred_element_type=F32)
+        dq = jnp.dot(ktbuf[...], grad_score, preferred_element_type=F32) * scaling
+        dq = jnp.transpose(dq).astype(BF16)
+
+        @pl.when(p == 0)
+        def _():
+            gp[b, at, :hd] = dq
+
+        @pl.when(p == 1)
+        def _():
+            gp[b, at, hd : 2 * hd] = dq
+
+        return carry
+
+    lax.fori_loop(0, q_rows // tile, attend, 0)
+    dkv[:, :, :, :hd] = (dkacc[...] * scaling).astype(BF16).reshape(n_pb, 2, q_half, hd)
+    dkv[:, :, :, hd:] = dvacc[...].astype(BF16).reshape(n_pb, 2, q_half, hd)
+    send(dkv.at[:, other], dkvp, "dk_p", 0, partner)
+    arrived(dkvp, "dk_p", 0)
+    dkvs[...] = (dkv[:, p].astype(F32) + dkvp[...].astype(F32)).astype(BF16)
+    for d in range(1, n_pb):
+        send(dkvs.at[lax.rem(b + d, n_pb)], dkvr.at[d], "dk_z", d, pb_dev(d))
+
+    def q_cols(pool):
+        return pl.ds(pl.multiple_of(pool * hd, hd), hd)
+
+    def half_rows(pool):
+        return pl.ds(pl.multiple_of(pool * q_half, q_half), q_half)
+
+    dq_own = gp.at[b, :, q_cols(p)]
+    send(dq_own, dq_own, "dq_p", 0, partner)
+    for d in range(1, n_pb):
+        send(dq_own, dq_own, "dq_z", d, pb_dev(d))
+
+    @pl.when(mine)
+    def _():
+        for d in range(1, n_ka):
+            region = xtbuf.at[:, :, ka_rows(k_from(d))]
+            arrived(region, "xt_ka", d)
+            remote(region, region, "xt_fw", d, partner).start()
+
+    total = dkvs[b].astype(F32)
+    for d in range(1, n_pb):
+        arrived(dkvr.at[d], "dk_z", d)
+        total += dkvr[d].astype(F32)
+    gp[b, half_rows(p), kv_at:] = total.astype(BF16)
+    kv_own = gp.at[b, half_rows(p), pl.ds(kv_at, 2 * hd)]
+    send(kv_own, kv_own, "gk_p", 0, partner)
+    for d in range(1, n_pb):
+        send(kv_own, kv_own, "gk_z", d, pb_dev(d))
+    arrived(gp.at[b, :, q_cols(other)], "dq_p", 0)
+    arrived(gp.at[b, half_rows(other), pl.ds(kv_at, 2 * hd)], "gk_p", 0)
+
+    mgp[b] = jnp.where(own_mask(b), gp[b].astype(F32), 0.0).astype(BF16)
+
+    def back_chunk(c, carry):
+        def product(pool):
+            at = pl.ds(pl.multiple_of(pool * half + c * chunk, 128), chunk)
+            return lax.dot_general(mgp[b], wbuf[at, :], NT, preferred_element_type=F32)
+
+        bsend[c] = product(other).astype(BF16)
+        remote(bsend.at[c], brecv.at[c], "bk_p", c, partner).start()
+        own = product(p).astype(BF16).astype(F32)
+        arrived(brecv.at[c], "bk_p", c)
+        bsum[c] = (own + brecv[c].astype(F32)).astype(BF16)
+        for d in range(1, n_ka):
+            remote(
+                bsum.at[c, ka_rows(lax.rem(k + d, n_ka))], kar.at[d, c],
+                "bk_ka", d * n_c + c, ka_dev(d),
+            ).start()
+        return carry
+
+    lax.fori_loop(0, n_c, back_chunk, 0)
+
+    for d in range(1, n_pb):
+        region = gp.at[b_from(d), :, q_cols(p)]
+        arrived(region, "dq_z", d)
+        send(region, region, "dq_p", d, partner)
+    for d in range(1, n_pb):
+        region = gp.at[b_from(d), half_rows(p), pl.ds(kv_at, 2 * hd)]
+        arrived(region, "gk_z", d)
+        send(region, region, "gk_p", d, partner)
+    for d in range(1, n_pb):
+        arrived(modbuf.at[b_from(d)], "mod", d)
+    for d in range(1, n_pb):
+        arrived(gp.at[b_from(d), :, q_cols(other)], "dq_p", d)
+        arrived(gp.at[b_from(d), half_rows(other), pl.ds(kv_at, 2 * hd)], "gk_p", d)
+        source = b_from(d)
+        mgp[source] = jnp.where(own_mask(source), gp[source].astype(F32), 0.0).astype(BF16)
+
+    @pl.when(jnp.logical_not(mine))
+    def _():
+        for d in range(n_ka):
+            arrived(xtbuf.at[:, :, ka_rows(k_from(d))], "xt_fw", d)
+
+    w_tile = divisor(slice_rows, 16, 512)
+
+    def weight_rows(t, carry):
+        at = pl.ds(pl.multiple_of(t * w_tile, 16), w_tile)
+        acc = jnp.dot(xtbuf[0, at, :], mgp[0], preferred_element_type=F32)
+        for i in range(1, n_pb):
+            acc += jnp.dot(xtbuf[i, at, :], mgp[i], preferred_element_type=F32)
+        out_weight[0, at, :] = acc
+        return carry
+
+    lax.fori_loop(0, slice_rows // w_tile, weight_rows, 0)
+
+    for c in range(n_c):
+        acc = bsum[c, ka_rows(k), :].astype(F32)
+        for d in range(1, n_ka):
+            arrived(kar.at[d, c], "bk_ka", d * n_c + c)
+            acc += kar[d, c].astype(F32)
+        out_tok[:, c * chunk : (c + 1) * chunk] = acc.astype(BF16)
+
+    for copy in sends:
+        copy.wait_send()
+    for d in range(1, n_pb):
+        target = lax.rem(b + d, n_pb)
+
+        @pl.when(lax.div(target, hp) == p)
+        def _(d=d):
+            remote(xt.at[0], xtbuf.at[b, :, ka_rows(k)], "xt_z", d, pb_dev(d)).wait_send()
+
+    @pl.when(mine)
+    def _():
+        region = xtbuf.at[:, :, ka_rows(k)]
+        for d in range(1, n_ka):
+            remote(region, region, "xt_ka", d, ka_dev(d)).wait_send()
+        for d in range(n_ka):
+            region = xtbuf.at[:, :, ka_rows(k_from(d))]
+            remote(region, region, "xt_fw", d, partner).wait_send()
+
+    def sent(c, carry):
+        remote(bsend.at[c], brecv.at[c], "bk_p", c, partner).wait_send()
+        for d in range(1, n_ka):
+            remote(
+                bsum.at[c, ka_rows(lax.rem(k + d, n_ka))], kar.at[d, c],
+                "bk_ka", d * n_c + c, ka_dev(d),
+            ).wait_send()
+        return carry
+
+    lax.fori_loop(0, n_c, sent, 0)
+
+
+def shards(tokens, modality, proj_weight, out_grad):
+    n_pool, n_pb, n_ka = (lax.axis_size(name) for name in ("pool", "pb", "ka"))
+    rows, half = tokens.shape
+    group = proj_weight.shape[2]
+    width = proj_weight.shape[1]
+    q_rows, hd = out_grad.shape[1:]
+    keys = n_pb * q_rows
+    slice_rows = width // n_pb
+    chunk = divisor(half, 128, 512)
+    n_c = half // chunk
+    vmem, scratch_bytes = [], 0
+    shapes = [
+        ((2, q_rows, half), BF16), ((width, group), BF16), ((n_pb, slice_rows, q_rows), BF16),
+        ((n_pb, q_rows, hd), BF16), ((q_rows, group), BF16), ((q_rows, group), BF16),
+        ((q_rows, hd), BF16), ((n_pb, 2, q_rows // 2, 2 * hd), BF16), ((hd, keys), BF16),
+        ((keys, hd), F32), ((keys, hd), F32), ((n_pb, 2, q_rows // 2, 2 * hd), BF16),
+        ((n_pb, q_rows // 2, 2 * hd), BF16), ((n_pb, q_rows // 2, 2 * hd), BF16),
+        ((n_pb, q_rows // 2, 2 * hd), BF16), ((n_pb, q_rows, group), BF16),
+        ((n_pb, q_rows, group), BF16), ((n_c, q_rows, chunk), BF16), ((n_c, q_rows, chunk), BF16),
+        ((n_c, q_rows, chunk), BF16), ((n_ka, n_c, rows, chunk), BF16),
+    ]
+    for shape, kind in shapes:
+        vmem.append(pltpu.VMEM(shape, kind))
+        scratch_bytes += math.prod(shape) * jnp.dtype(kind).itemsize
+    scratch_bytes += 5 * keys * min(256, q_rows) * 4 + slice_rows * group * 4
+    if scratch_bytes > 58 * 2**20 or n_pool != 2 or n_pb % 2:
+        return plain_shards(tokens, modality, proj_weight, out_grad)
+    offsets, count = {}, 0
+    for name, size in (
+        ("tok_ka", n_ka), ("tok_fw", n_ka), ("mod", n_pb), ("xt_z", n_pb), ("xt_ka", n_ka),
+        ("xt_fw", n_ka), ("pj", 1), ("kv_z", n_pb), ("kv_fw", n_pb), ("dk_p", 1), ("dk_z", n_pb),
+        ("dq_p", n_pb), ("dq_z", n_pb), ("gk_p", n_pb), ("gk_z", n_pb), ("bk_p", n_c),
+        ("bk_ka", n_ka * n_c),
+    ):
+        offsets[name] = count
+        count += size
+    dims = (n_pb, n_ka, rows, half, group, hd, q_rows, offsets)
+    in_vmem = pl.BlockSpec(memory_space=pltpu.VMEM)
+    turned = tokens.T.reshape(n_pb // 2, slice_rows, rows)
+    kinds = jnp.broadcast_to(modality.astype(BF16)[:, None], (q_rows, hd))
+    return pl.pallas_call(
+        functools.partial(fused, dims),
+        out_shape=(
+            jax.ShapeDtypeStruct((rows, half), BF16),
+            jax.ShapeDtypeStruct((1, slice_rows, group), F32),
+        ),
+        in_specs=[in_vmem, in_vmem, in_vmem, pl.BlockSpec(memory_space=pl.ANY), in_vmem],
+        out_specs=(in_vmem, in_vmem),
+        scratch_shapes=vmem
+        + [
+            pltpu.SemaphoreType.DMA,
+            pltpu.SemaphoreType.DMA((count,)),
+            pltpu.SemaphoreType.DMA((count,)),
+        ],
+        compiler_params=pltpu.CompilerParams(
+            collective_id=0, has_side_effects=True, vmem_limit_bytes=62 * 2**20
+        ),
+    )(tokens, turned, kinds, proj_weight, out_grad)
+
+
 def solution(mesh):
     return jax.shard_map(
         shards,

time: 343 us -> 131 us (0.38)
  waiting for transfers between devices: 275 us -> 0 us
  Pallas kernels: 0 us -> 120 us
  matrix products: 29.8 us -> 0 us
  between operations: 14.2 us -> 0.64 us
  other arithmetic: 6.9 us -> 0.69 us
  blocking collectives: 4.19 us -> 0 us
    reduce_scatter x3 -> x0, waiting for transfers between devices: 181 us -> none  [the longest x1 91.8 us: shards(): lax.psum_scatter(term.astype(jnp.bfloat16), 'pb', scatter_dimension=0, ti...]
    pallas_call x0 -> x1, Pallas kernels: none -> 120 us  [shards(): pl.pallas_call(functools.partial(fused, dims), out_shape=(jax.ShapeDtypeS...]
    all_gather x2 -> x0, waiting for transfers between devices: 74 us -> none  [the longest x1 44.6 us: shards(): gathered = lax.all_gather(tokens[None], ('pool', 'ka'), axis=0, tiled=True)]
    dot_general x8 -> x0, matrix products: 29.8 us -> none  [the longest x1 7.99 us: shards(): lax.dot_general(block_tokens, weight, (((0, 2), (0, 1)), ((), ())), prefe...]
    psum x1 -> x0, waiting for transfers between devices: 19.1 us -> none  [shards(): projected = lax.psum(local_proj.astype(jnp.bfloat16), 'pool')]
    convert_element_type x1 -> x0, local copies, waits for them, and re-layouts: 8.28 us -> none  [shards(): term.astype(jnp.bfloat16)]
    unnamed x4 -> x2, local copies, waits for them, and re-layouts: 0.01 us -> 5.56 us
    all_gather x2 -> x0, blocking collectives: 4.19 us -> none  [the longest x1 2.19 us: shards(): lax.all_gather(key_cell, 'pool', axis=0, tiled=True)]
  transfers between devices with their start and end apart: 6 -> 0, of which waited for: 6 -> 0; matrix products, arithmetic and copies ran while one was open for 4% -> 0% of each run, Pallas kernels for 0% -> 0%
where the time goes in v1:
time: 131 us; the launch traced here: 130 us
  Pallas kernels  120 us (92%)
  local copies, waits for them, and re-layouts  8.57 us (7%)
    pallas_call x1, Pallas kernels, shards(): pl.pallas_call(functools.partial(fused, dims), out_shape=(jax.ShapeDtypeS...  120 us
    unnamed x2, local copies, waits for them, and re-layouts  5.56 us

profile of v1, /device:TPU:10, one launch (start us, length us, event | category | flops | bytes accessed | tf_op | source)
XLA Modules:
  0.0 129.8 jit_solution(14454980476686842431)
XLA Ops:
  0.6 0.7 convert_element_type.3
  1.3 0.8 broadcast_in_dim.2.mod
  2.1 2.2 %copy.6 = bf16[2688,128]{1,0:T(8,128)(2,1)} copy(bf16[2688,128]{0,1:T(8,128)(2,1)} %bitcast.2) | data formatting | bytes 1376256 | tf_op jit(solution)/shard_map/transpose | solution.py:440
  4.3 119.9 %shard_map.59 = (bf16[128,2688]{1,0:T(8,128)(2,1)}, f32[1,1344,512]{2,1,0:T(8,128)}) custom-call(bf16[128,2688]{1,0:T(8,128)(2,1)} %tok.1, bf16[2,1344,128]{2,1,0:T(8,128)(2,1)} %bitcast.3, bf16[512,128]{1,0:T(8,128)(2,1)} %broadcast_in_dim.2.mod, bf16[1,5376,512]{2,1,0:T(8,128)(2,1)} %weight_hbm.1, bf16[1,512,128]{2,1,0:T(8,128)(2,1)} %cot.1), custom_call_target="tpu_custom_call" | custom-call | tf_op jit(solution)/shard_map/pallas_call | solution.py:442
  124.2 2.0 %copy.9 = bf16[128,2688]{1,0:T(8,128)(2,1)} copy(bf16[128,2688]{1,0:T(8,128)(2,1)} %get-tuple-element.4) | data formatting | bytes 1376256
  126.2 3.6 %copy.10 = f32[1,1344,512]{2,1,0:T(8,128)} copy(f32[1,1344,512]{2,1,0:T(8,128)} %get-tuple-element.5) | data formatting | bytes 5505024

commit v2 on v1

--- a/solution.py
+++ b/solution.py
@@ -117,9 +117,9 @@
 
 
 def fused(
-    dims, tok, xt, mod, weight_hbm, cot, out_tok, out_weight,
-    tokbuf, wbuf, xtbuf, modbuf, projloc, projrecv, qbuf, kvbuf, ktbuf, dkacc, dvacc,
-    dkv, dkvp, dkvs, dkvr, gp, mgp, bsend, brecv, bsum, kar, load_sem, ss, rs,
+    dims, tok, mod, weight_hbm, cot, out_tok, out_weight,
+    tokbuf, wbuf, xtbuf, modbuf, projloc, projrecv, qbuf, kvbuf, ktbuf, prob, score,
+    dkv, dkvp, dkvs, dkvr, gp, mgp, bsend, brecv, bsum, kar, rel, xt, wout, load_sem, store_sem, ss, rs,
 ):
     n_pb, n_ka, rows, half, group, hd, q_rows, offsets = dims
     scaling = 1.0 / math.sqrt(hd)
@@ -128,7 +128,15 @@
     q_half = q_rows // 2
     hp = n_pb // 2
     n_c, chunk = bsend.shape[0], bsend.shape[2]
-    slice_rows = xt.shape[1]
+    slice_rows = xtbuf.shape[1]
+    part = rows // 2
+    low, high_bit = lax.rem(k, 2), lax.div(k, 2)
+    near = [
+        k,
+        2 * high_bit + 1 - low,
+        2 * (1 - high_bit) + low,
+        2 * (1 - high_bit) + 1 - low,
+    ]
     kv_at = group - 2 * hd
     partner = (other, b, k)
     sends = []
@@ -171,11 +179,26 @@
     load.start()
     pl.semaphore_wait(barrier, len(devs))
 
-    for d in range(1, n_ka):
-        send(tok, tokbuf.at[p, ka_rows(k)], "tok_ka", d, ka_dev(d))
-    send(tok, tokbuf.at[p, ka_rows(k)], "tok_fw", 0, partner)
+    def tok_part(pool, source, h):
+        return tokbuf.at[pool, pl.ds(pl.multiple_of(source * rows + h * part, part), part)]
+
+    for e, h in ((1, 0), (2, 1), (1, 1), (2, 0)):
+        send(
+            tok.at[pl.ds(h * part, part)], tok_part(p, k, h), "tok_ka", 2 * e + h, (p, b, near[e])
+        )
+    for h in range(2):
+        send(tok.at[pl.ds(h * part, part)], tok_part(p, k, h), "tok_fw", h, partner)
     for d in range(1, n_pb):
         send(mod, modbuf.at[b], "mod", d, pb_dev(d))
+    tokbuf[p, ka_rows(k), :] = tok[...]
+    modbuf[b] = mod[...]
+
+    for i in range(half // 128):
+        cols = slice(i * 128, (i + 1) * 128)
+        xt[cols, :] = jnp.transpose(tok[:, cols].astype(F32)).astype(BF16)
+
+    def xt_part(target):
+        return pl.ds(pl.multiple_of(lax.rem(target, hp) * slice_rows, 16), slice_rows)
 
     mine = lax.div(b, hp) == p
     for d in range(1, n_pb):
@@ -184,31 +207,64 @@
         @pl.when(lax.div(target, hp) == p)
         def _(d=d, target=target):
             remote(
-                xt.at[lax.rem(target, hp)], xtbuf.at[b, :, ka_rows(k)], "xt_z", d, pb_dev(d)
+                xt.at[xt_part(target)], xtbuf.at[b, :, ka_rows(k)], "xt_z", d, pb_dev(d)
             ).start()
 
-    tokbuf[p, ka_rows(k), :] = tok[...]
-    modbuf[b] = mod[...]
-
     @pl.when(mine)
     def _():
-        xtbuf[b, :, ka_rows(k)] = xt[lax.rem(b, hp)]
-
-    for d in range(1, n_ka):
-        region = tokbuf.at[p, ka_rows(k_from(d))]
-        arrived(region, "tok_ka", d)
-        send(region, region, "tok_fw", d, partner)
-    for d in range(n_ka):
-        arrived(tokbuf.at[other, ka_rows(k_from(d))], "tok_fw", d)
-    load.wait()
+        xtbuf[b, :, ka_rows(k)] = xt[xt_part(b), :]
 
     def own_mask(index):
         return modbuf[index].astype(F32)[:, :1] == p.astype(F32)
 
-    proj = jnp.dot(tokbuf[0], wbuf[:half], preferred_element_type=F32)
-    proj += jnp.dot(tokbuf[1], wbuf[half:], preferred_element_type=F32)
-    projloc[...] = proj.astype(BF16)
-    send(projloc, projrecv, "pj", 0, partner)
+    def hand_on(e, h, relay_to):
+        region = tok_part(p, near[e], h)
+        arrived(region, "tok_ka", 2 * e + h)
+        if relay_to is not None:
+            send(region, region, "tok_ka", 6 + h, (p, b, near[relay_to]))
+        send(region, region, "tok_fw", 2 * e + h, partner)
+
+    def project(e):
+        for h in range(2):
+            arrived(tok_part(other, near[e], h), "tok_fw", 2 * e + h)
+        at = ka_rows(near[e])
+        proj = jnp.dot(tokbuf[0, at, :], wbuf[:half], preferred_element_type=F32)
+        proj += jnp.dot(tokbuf[1, at, :], wbuf[half:], preferred_element_type=F32)
+        projloc[at, :] = proj.astype(BF16)
+        send(projloc.at[at], projrecv.at[at], "pj", e, partner)
+
+    def settle(e):
+        at = ka_rows(near[e])
+        arrived(projrecv.at[at], "pj", e)
+        owned = modbuf[b, at, :].astype(F32)[:, :1] == p.astype(F32)
+        projected = jnp.where(owned, projloc[at, :].astype(F32), projrecv[at, :].astype(F32))
+        qbuf[at, :] = jnp.where(p == 0, projected[:, :hd], projected[:, hd : 2 * hd]).astype(BF16)
+        kvbuf[b, near[e]] = projected[:, kv_at:].astype(BF16).reshape(2, part, 2 * hd)
+        region = kvbuf.at[b, near[e], p]
+        for d in range(1, n_pb):
+            send(region, region, "kv_z", d * n_ka + e, pb_dev(d))
+
+    def pass_keys(e):
+        for d in range(1, n_pb):
+            region = kvbuf.at[b_from(d), near[e], p]
+            arrived(region, "kv_z", d * n_ka + e)
+            send(region, region, "kv_fw", d * n_ka + e, partner)
+
+    load.wait()
+    project(0)
+    hand_on(1, 0, 2)
+    hand_on(2, 1, 1)
+    settle(0)
+    hand_on(1, 1, None)
+    hand_on(2, 0, None)
+    project(1)
+    project(2)
+    settle(1)
+    settle(2)
+    pass_keys(0)
+    hand_on(3, 0, None)
+    hand_on(3, 1, None)
+    project(3)
 
     @pl.when(mine)
     def _():
@@ -220,63 +276,62 @@
         region = xtbuf.at[:, :, ka_rows(k)]
         remote(region, region, "xt_fw", 0, partner).start()
 
-    arrived(projrecv, "pj", 0)
-    projected = jnp.where(own_mask(b), projloc[...].astype(F32), projrecv[...].astype(F32)).astype(BF16)
-    qbuf[...] = jnp.where(p == 0, projected[:, :hd].astype(F32), projected[:, hd : 2 * hd].astype(F32)).astype(BF16)
-    kvbuf[b] = projected[:, kv_at:].reshape(2, q_half, 2 * hd)
-    for d in range(1, n_pb):
-        send(kvbuf.at[b, p], kvbuf.at[b, p], "kv_z", d, pb_dev(d))
-    for d in range(1, n_pb):
-        region = kvbuf.at[b_from(d), p]
-        arrived(region, "kv_z", d)
-        send(region, region, "kv_fw", d, partner)
-    for d in range(1, n_pb):
-        arrived(kvbuf.at[b_from(d), other], "kv_fw", d)
+    settle(3)
+    for e in range(1, n_ka):
+        pass_keys(e)
+    for e in range(n_ka):
+        for d in range(1, n_pb):
+            arrived(kvbuf.at[b_from(d), near[e], other], "kv_fw", d * n_ka + e)
 
     keys = n_pb * q_rows
-    ktbuf[...] = jnp.transpose(
-        kvbuf[:, :, :, :hd].reshape(keys, hd).astype(F32)
-    ).astype(BF16)
-    dkacc[...] = jnp.zeros_like(dkacc)
-    dvacc[...] = jnp.zeros_like(dvacc)
+    key_rows = kvbuf[:, :, :, :, :hd].reshape(keys, hd)
+    ktbuf[...] = jnp.transpose(key_rows.astype(F32)).astype(BF16)
     tile = min(256, q_rows)
-
-    def attend(t, carry):
-        at = pl.ds(pl.multiple_of(t * tile, tile), tile)
-        q = qbuf[at, :]
-        o = cot[0, at, :]
-        key_rows = kvbuf[:, :, :, :hd].reshape(keys, hd)
-        value_rows = kvbuf[:, :, :, hd:].reshape(keys, hd)
-        scores = lax.dot_general(key_rows, q, NT, preferred_element_type=F32) * scaling
+    for t in range(q_rows // tile):
+        at = slice(t * tile, (t + 1) * tile)
+        key_rows = kvbuf[:, :, :, :, :hd].reshape(keys, hd)
+        value_rows = kvbuf[:, :, :, :, hd:].reshape(keys, hd)
+        scores = lax.dot_general(key_rows, qbuf[at, :], NT, preferred_element_type=F32) * scaling
         high = jnp.max(scores, axis=0, keepdims=True)
         raised = jnp.exp(scores - high)
         softmax = raised * (1.0 / jnp.sum(raised, axis=0, keepdims=True))
-        grad_prob = lax.dot_general(value_rows, o, NT, preferred_element_type=F32)
+        grad_prob = lax.dot_general(value_rows, cot[0, at, :], NT, preferred_element_type=F32)
         delta = jnp.sum(softmax * grad_prob, axis=0, keepdims=True)
         grad_score = (softmax * (grad_prob - delta)).astype(BF16)
-        dkacc[...] += jnp.dot(grad_score, q, preferred_element_type=F32)
-        dvacc[...] += jnp.dot(softmax.astype(BF16), o, preferred_element_type=F32)
-        dq = jnp.dot(ktbuf[...], grad_score, preferred_element_type=F32) * scaling
-        dq = jnp.transpose(dq).astype(BF16)
-
-        @pl.when(p == 0)
-        def _():
-            gp[b, at, :hd] = dq
-
-        @pl.when(p == 1)
-        def _():
-            gp[b, at, hd : 2 * hd] = dq
-
-        return carry
-
-    lax.fori_loop(0, q_rows // tile, attend, 0)
-    dkv[:, :, :, :hd] = (dkacc[...] * scaling).astype(BF16).reshape(n_pb, 2, q_half, hd)
-    dkv[:, :, :, hd:] = dvacc[...].astype(BF16).reshape(n_pb, 2, q_half, hd)
-    send(dkv.at[:, other], dkvp, "dk_p", 0, partner)
-    arrived(dkvp, "dk_p", 0)
-    dkvs[...] = (dkv[:, p].astype(F32) + dkvp[...].astype(F32)).astype(BF16)
-    for d in range(1, n_pb):
-        send(dkvs.at[lax.rem(b + d, n_pb)], dkvr.at[d], "dk_z", d, pb_dev(d))
+        prob[:, :, at] = softmax.astype(BF16).reshape(n_pb, q_rows, tile)
+        score[:, :, at] = grad_score.reshape(n_pb, q_rows, tile)
+
+    def key_block(d):
+        block = lax.rem(b + d, n_pb)
+        dk = jnp.dot(score[block], qbuf[...], preferred_element_type=F32) * scaling
+        dv = jnp.dot(prob[block], cot[0], preferred_element_type=F32)
+        dkv[block, :, :, :hd] = dk.astype(BF16).reshape(2, q_half, hd)
+        dkv[block, :, :, hd:] = dv.astype(BF16).reshape(2, q_half, hd)
+        send(dkv.at[block, other], dkvp.at[block], "dk_p", d, partner)
+
+    def key_sum(d):
+        block = lax.rem(b + d, n_pb)
+        arrived(dkvp.at[block], "dk_p", d)
+        dkvs[block] = (dkv[block, p].astype(F32) + dkvp[block].astype(F32)).astype(BF16)
+        if d:
+            send(dkvs.at[block], dkvr.at[d], "dk_z", d, pb_dev(d))
+
+    turns = list(range(1, n_pb)) + [0]
+    for i, d in enumerate(turns):
+        key_block(d)
+        if i:
+            key_sum(turns[i - 1])
+    key_sum(0)
+    dq = jnp.dot(ktbuf[...], score[...].reshape(keys, q_rows), preferred_element_type=F32) * scaling
+    dq = jnp.transpose(dq).astype(BF16)
+
+    @pl.when(p == 0)
+    def _():
+        gp[b, :, :hd] = dq
+
+    @pl.when(p == 1)
+    def _():
+        gp[b, :, hd : 2 * hd] = dq
 
     def q_cols(pool):
         return pl.ds(pl.multiple_of(pool * hd, hd), hd)
@@ -310,6 +365,24 @@
 
     mgp[b] = jnp.where(own_mask(b), gp[b].astype(F32), 0.0).astype(BF16)
 
+    def relayed(e, c):
+        h = 2 - e
+        arrived(rel.at[h, c], "rel", h * n_c + c)
+        at = pl.ds(pl.multiple_of(near[e] * rows + h * part, part), part)
+        bsum[c, at, :] = (bsum[c, at, :].astype(F32) + rel[h, c].astype(F32)).astype(BF16)
+        return partial_copy(e, h, c)
+
+    def partial_copy(e, h, c):
+        at = pl.ds(pl.multiple_of(near[e] * rows + h * part, part), part)
+        return remote(
+            bsum.at[c, at], kar.at[e - 1, c, pl.ds(h * part, part)],
+            "kar", (2 * (e - 1) + h) * n_c + c, (p, b, near[e]),
+        )
+
+    def relay_copy(h, c):
+        at = pl.ds(pl.multiple_of(near[3] * rows + h * part, part), part)
+        return remote(bsum.at[c, at], rel.at[h, c], "rel", h * n_c + c, (p, b, near[1 + h]))
+
     def back_chunk(c, carry):
         def product(pool):
             at = pl.ds(pl.multiple_of(pool * half + c * chunk, 128), chunk)
@@ -320,14 +393,21 @@
         own = product(p).astype(BF16).astype(F32)
         arrived(brecv.at[c], "bk_p", c)
         bsum[c] = (own + brecv[c].astype(F32)).astype(BF16)
-        for d in range(1, n_ka):
-            remote(
-                bsum.at[c, ka_rows(lax.rem(k + d, n_ka))], kar.at[d, c],
-                "bk_ka", d * n_c + c, ka_dev(d),
-            ).start()
+        for h in range(2):
+            relay_copy(h, c).start()
+        partial_copy(1, 0, c).start()
+        partial_copy(2, 1, c).start()
+
+        @pl.when(c > 0)
+        def _():
+            for e in (2, 1):
+                relayed(e, c - 1).start()
+
         return carry
 
     lax.fori_loop(0, n_c, back_chunk, 0)
+    for e in (2, 1):
+        relayed(e, n_c - 1).start()
 
     for d in range(1, n_pb):
         region = gp.at[b_from(d), :, q_cols(p)]
@@ -357,26 +437,30 @@
         acc = jnp.dot(xtbuf[0, at, :], mgp[0], preferred_element_type=F32)
         for i in range(1, n_pb):
             acc += jnp.dot(xtbuf[i, at, :], mgp[i], preferred_element_type=F32)
-        out_weight[0, at, :] = acc
+        wout[at, :] = acc
         return carry
 
     lax.fori_loop(0, slice_rows // w_tile, weight_rows, 0)
+    store = pltpu.make_async_copy(wout, out_weight.at[0], store_sem)
+    store.start()
 
     for c in range(n_c):
         acc = bsum[c, ka_rows(k), :].astype(F32)
-        for d in range(1, n_ka):
-            arrived(kar.at[d, c], "bk_ka", d * n_c + c)
-            acc += kar[d, c].astype(F32)
+        for e in (1, 2):
+            for h in range(2):
+                arrived(kar.at[e - 1, c, pl.ds(h * part, part)], "kar", (2 * (e - 1) + h) * n_c + c)
+            acc += kar[e - 1, c].astype(F32)
         out_tok[:, c * chunk : (c + 1) * chunk] = acc.astype(BF16)
 
+    store.wait()
     for copy in sends:
         copy.wait_send()
     for d in range(1, n_pb):
         target = lax.rem(b + d, n_pb)
 
         @pl.when(lax.div(target, hp) == p)
-        def _(d=d):
-            remote(xt.at[0], xtbuf.at[b, :, ka_rows(k)], "xt_z", d, pb_dev(d)).wait_send()
+        def _(d=d, target=target):
+            remote(xt.at[xt_part(target)], xtbuf.at[b, :, ka_rows(k)], "xt_z", d, pb_dev(d)).wait_send()
 
     @pl.when(mine)
     def _():
@@ -389,11 +473,10 @@
 
     def sent(c, carry):
         remote(bsend.at[c], brecv.at[c], "bk_p", c, partner).wait_send()
-        for d in range(1, n_ka):
-            remote(
-                bsum.at[c, ka_rows(lax.rem(k + d, n_ka))], kar.at[d, c],
-                "bk_ka", d * n_c + c, ka_dev(d),
-            ).wait_send()
+        for h in range(2):
+            relay_copy(h, c).wait_send()
+            for e in (1, 2):
+                partial_copy(e, h, c).wait_send()
         return carry
 
     lax.fori_loop(0, n_c, sent, 0)
@@ -413,31 +496,31 @@
     shapes = [
         ((2, q_rows, half), BF16), ((width, group), BF16), ((n_pb, slice_rows, q_rows), BF16),
         ((n_pb, q_rows, hd), BF16), ((q_rows, group), BF16), ((q_rows, group), BF16),
-        ((q_rows, hd), BF16), ((n_pb, 2, q_rows // 2, 2 * hd), BF16), ((hd, keys), BF16),
-        ((keys, hd), F32), ((keys, hd), F32), ((n_pb, 2, q_rows // 2, 2 * hd), BF16),
+        ((q_rows, hd), BF16), ((n_pb, n_ka, 2, rows // 2, 2 * hd), BF16), ((hd, keys), BF16),
+        ((n_pb, q_rows, q_rows), BF16), ((n_pb, q_rows, q_rows), BF16), ((n_pb, 2, q_rows // 2, 2 * hd), BF16),
         ((n_pb, q_rows // 2, 2 * hd), BF16), ((n_pb, q_rows // 2, 2 * hd), BF16),
         ((n_pb, q_rows // 2, 2 * hd), BF16), ((n_pb, q_rows, group), BF16),
         ((n_pb, q_rows, group), BF16), ((n_c, q_rows, chunk), BF16), ((n_c, q_rows, chunk), BF16),
-        ((n_c, q_rows, chunk), BF16), ((n_ka, n_c, rows, chunk), BF16),
+        ((n_c, q_rows, chunk), BF16), ((2, n_c, rows, chunk), BF16),
+        ((2, n_c, rows // 2, chunk), BF16), ((half, rows), BF16), ((slice_rows, group), F32),
     ]
     for shape, kind in shapes:
         vmem.append(pltpu.VMEM(shape, kind))
         scratch_bytes += math.prod(shape) * jnp.dtype(kind).itemsize
-    scratch_bytes += 5 * keys * min(256, q_rows) * 4 + slice_rows * group * 4
-    if scratch_bytes > 58 * 2**20 or n_pool != 2 or n_pb % 2:
+    scratch_bytes += 5 * keys * min(256, q_rows) * 4
+    if scratch_bytes > 58 * 2**20 or n_pool != 2 or n_pb % 2 or n_ka != 4:
         return plain_shards(tokens, modality, proj_weight, out_grad)
     offsets, count = {}, 0
     for name, size in (
-        ("tok_ka", n_ka), ("tok_fw", n_ka), ("mod", n_pb), ("xt_z", n_pb), ("xt_ka", n_ka),
-        ("xt_fw", n_ka), ("pj", 1), ("kv_z", n_pb), ("kv_fw", n_pb), ("dk_p", 1), ("dk_z", n_pb),
+        ("tok_ka", 2 * n_ka), ("tok_fw", 2 * n_ka), ("mod", n_pb), ("xt_z", n_pb), ("xt_ka", n_ka),
+        ("xt_fw", n_ka), ("pj", n_ka), ("kv_z", n_pb * n_ka), ("kv_fw", n_pb * n_ka), ("dk_p", n_pb), ("dk_z", n_pb),
         ("dq_p", n_pb), ("dq_z", n_pb), ("gk_p", n_pb), ("gk_z", n_pb), ("bk_p", n_c),
-        ("bk_ka", n_ka * n_c),
+        ("kar", 4 * n_c), ("rel", 2 * n_c),
     ):
         offsets[name] = count
         count += size
     dims = (n_pb, n_ka, rows, half, group, hd, q_rows, offsets)
     in_vmem = pl.BlockSpec(memory_space=pltpu.VMEM)
-    turned = tokens.T.reshape(n_pb // 2, slice_rows, rows)
     kinds = jnp.broadcast_to(modality.astype(BF16)[:, None], (q_rows, hd))
     return pl.pallas_call(
         functools.partial(fused, dims),
@@ -445,10 +528,11 @@
             jax.ShapeDtypeStruct((rows, half), BF16),
             jax.ShapeDtypeStruct((1, slice_rows, group), F32),
         ),
-        in_specs=[in_vmem, in_vmem, in_vmem, pl.BlockSpec(memory_space=pl.ANY), in_vmem],
-        out_specs=(in_vmem, in_vmem),
+        in_specs=[in_vmem, in_vmem, pl.BlockSpec(memory_space=pl.ANY), in_vmem],
+        out_specs=(in_vmem, pl.BlockSpec(memory_space=pl.ANY)),
         scratch_shapes=vmem
         + [
+            pltpu.SemaphoreType.DMA,
             pltpu.SemaphoreType.DMA,
             pltpu.SemaphoreType.DMA((count,)),
             pltpu.SemaphoreType.DMA((count,)),
@@ -456,7 +540,7 @@
         compiler_params=pltpu.CompilerParams(
             collective_id=0, has_side_effects=True, vmem_limit_bytes=62 * 2**20
         ),
-    )(tokens, turned, kinds, proj_weight, out_grad)
+    )(tokens, kinds, proj_weight, out_grad)
 
 
 def solution(mesh):

time: 131 us -> 120 us (0.916)
  the two profiles are of different devices: /device:TPU:10 before, /device:TPU:0 now
where the time goes in v2:
time: 120 us
  Pallas kernels  112 us (93%)
  local copies, waits for them, and re-layouts  6.35 us (5%)
    pallas_call x1, Pallas kernels, shards(): pl.pallas_call(functools.partial(fused, dims), out_shape=(jax.ShapeDtypeS...  112 us
    unnamed x2, local copies, waits for them, and re-layouts  5.56 us

profile of v2, /device:TPU:0, one launch (start us, length us, event | category | flops | bytes accessed | tf_op | source)
XLA Modules:
  0.0 119.8 jit_solution(16653938154480848335)
XLA Ops:
  0.6 0.7 convert_element_type.3
  1.3 0.8 broadcast_in_dim.2.mod
  2.1 112.1 %shard_map.59 = (bf16[128,2688]{1,0:T(8,128)(2,1)}, f32[1,1344,512]{2,1,0:T(8,128)}) custom-call(bf16[128,2688]{1,0:T(8,128)(2,1)} %tok.1, bf16[512,128]{1,0:T(8,128)(2,1)} %broadcast_in_dim.2.mod, bf16[1,5376,512]{2,1,0:T(8,128)(2,1)} %weight_hbm.1, bf16[1,512,128]{2,1,0:T(8,128)(2,1)} %cot.1), custom_call_target="tpu_custom_call" | custom-call | tf_op jit(solution)/shard_map/pallas_call | solution.py:525
  114.2 2.0 %copy.8 = bf16[128,2688]{1,0:T(8,128)(2,1)} copy(bf16[128,2688]{1,0:T(8,128)(2,1)} %get-tuple-element.4) | data formatting | bytes 1376256
  116.2 3.6 %copy.9 = f32[1,1344,512]{2,1,0:T(8,128)} copy(f32[1,1344,512]{2,1,0:T(8,128)} %get-tuple-element.5) | data formatting | bytes 5505024

commit v3 on v2

--- a/solution.py
+++ b/solution.py
@@ -291,9 +291,9 @@
         at = slice(t * tile, (t + 1) * tile)
         key_rows = kvbuf[:, :, :, :, :hd].reshape(keys, hd)
         value_rows = kvbuf[:, :, :, :, hd:].reshape(keys, hd)
-        scores = lax.dot_general(key_rows, qbuf[at, :], NT, preferred_element_type=F32) * scaling
+        scores = lax.dot_general(key_rows, qbuf[at, :], NT, preferred_element_type=F32)
         high = jnp.max(scores, axis=0, keepdims=True)
-        raised = jnp.exp(scores - high)
+        raised = jnp.exp((scores - high) * scaling)
         softmax = raised * (1.0 / jnp.sum(raised, axis=0, keepdims=True))
         grad_prob = lax.dot_general(value_rows, cot[0, at, :], NT, preferred_element_type=F32)
         delta = jnp.sum(softmax * grad_prob, axis=0, keepdims=True)
@@ -390,24 +390,29 @@
 
         bsend[c] = product(other).astype(BF16)
         remote(bsend.at[c], brecv.at[c], "bk_p", c, partner).start()
-        own = product(p).astype(BF16).astype(F32)
+        bsum[c] = product(p).astype(BF16)
+
+        @pl.when(c > 0)
+        def _():
+            pool_sum(c - 1)
+
+        return carry
+
+    def pool_sum(c):
         arrived(brecv.at[c], "bk_p", c)
-        bsum[c] = (own + brecv[c].astype(F32)).astype(BF16)
+        bsum[c] = (bsum[c].astype(F32) + brecv[c].astype(F32)).astype(BF16)
         for h in range(2):
             relay_copy(h, c).start()
         partial_copy(1, 0, c).start()
         partial_copy(2, 1, c).start()
 
-        @pl.when(c > 0)
-        def _():
-            for e in (2, 1):
-                relayed(e, c - 1).start()
-
-        return carry
+    def relay_sums(c):
+        for e in (2, 1):
+            relayed(e, c).start()
 
     lax.fori_loop(0, n_c, back_chunk, 0)
-    for e in (2, 1):
-        relayed(e, n_c - 1).start()
+    pool_sum(n_c - 1)
+    relay_sums(0)
 
     for d in range(1, n_pb):
         region = gp.at[b_from(d), :, q_cols(p)]
@@ -430,17 +435,28 @@
         for d in range(n_ka):
             arrived(xtbuf.at[:, :, ka_rows(k_from(d))], "xt_fw", d)
 
-    w_tile = divisor(slice_rows, 16, 512)
-
-    def weight_rows(t, carry):
+    tiles = n_c - 1 if n_c > 1 and slice_rows % (16 * (n_c - 1)) == 0 else 1
+    w_tile = slice_rows // tiles
+
+    def weight_rows(t):
         at = pl.ds(pl.multiple_of(t * w_tile, 16), w_tile)
         acc = jnp.dot(xtbuf[0, at, :], mgp[0], preferred_element_type=F32)
         for i in range(1, n_pb):
             acc += jnp.dot(xtbuf[i, at, :], mgp[i], preferred_element_type=F32)
         wout[at, :] = acc
+
+    def weight_and_relay(t, carry):
+        relay_sums(t + 1)
+
+        @pl.when(t < tiles)
+        def _():
+            weight_rows(t)
+
         return carry
 
-    lax.fori_loop(0, slice_rows // w_tile, weight_rows, 0)
+    lax.fori_loop(0, n_c - 1, weight_and_relay, 0)
+    if n_c == 1:
+        weight_rows(0)
     store = pltpu.make_async_copy(wout, out_weight.at[0], store_sem)
     store.start()
 
@@ -480,6 +496,25 @@
         return carry
 
     lax.fori_loop(0, n_c, sent, 0)
+
+
+def hand_over(tok_from, weight_from, tok_to, weight_to, sems):
+    count = sems.shape[0]
+    copies = []
+    for source, target, first, parts in (
+        (tok_from, tok_to, 0, 2),
+        (weight_from.at[0], weight_to.at[0], 2, count - 2),
+    ):
+        if source.shape[0] % (8 * parts * 2):
+            parts = 1
+        rows = source.shape[0] // parts
+        for i in range(parts):
+            at = pl.ds(i * rows, rows)
+            copies.append(pltpu.make_async_copy(source.at[at], target.at[at], sems.at[first + i]))
+    for copy in copies:
+        copy.start()
+    for copy in copies:
+        copy.wait()
 
 
 def shards(tokens, modality, proj_weight, out_grad):
@@ -522,7 +557,7 @@
     dims = (n_pb, n_ka, rows, half, group, hd, q_rows, offsets)
     in_vmem = pl.BlockSpec(memory_space=pltpu.VMEM)
     kinds = jnp.broadcast_to(modality.astype(BF16)[:, None], (q_rows, hd))
-    return pl.pallas_call(
+    made = pl.pallas_call(
         functools.partial(fused, dims),
         out_shape=(
             jax.ShapeDtypeStruct((rows, half), BF16),
@@ -541,6 +576,15 @@
             collective_id=0, has_side_effects=True, vmem_limit_bytes=62 * 2**20
         ),
     )(tokens, kinds, proj_weight, out_grad)
+    any_space = pl.BlockSpec(memory_space=pl.ANY)
+    return pl.pallas_call(
+        hand_over,
+        out_shape=tuple(jax.ShapeDtypeStruct(x.shape, x.dtype) for x in made),
+        in_specs=[any_space, any_space],
+        out_specs=(any_space, any_space),
+        scratch_shapes=[pltpu.SemaphoreType.DMA((8,))],
+        compiler_params=pltpu.CompilerParams(vmem_limit_bytes=62 * 2**20),
+    )(*made)
 
 
 def solution(mesh):

time: 120 us -> 217 us (1.81)
  the two profiles are of different devices: /device:TPU:0 before, /device:TPU:10 now
where the time goes in v3:
time: 217 us; the launch traced here: 214 us
  Pallas kernels  211 us (97%)
    pallas_call x1, Pallas kernels, shards(): pl.pallas_call(functools.partial(fused, dims), out_shape=(jax.ShapeDtypeS...  106 us
    pallas_call x1, Pallas kernels, shards(): pl.pallas_call(hand_over, out_shape=tuple((jax.ShapeDtypeStruct(x.shape,...  105 us

profile of v3, /device:TPU:10, one launch (start us, length us, event | category | flops | bytes accessed | tf_op | source)
XLA Modules:
  0.0 213.5 jit_solution(8119258625714125357)
XLA Ops:
  0.6 0.7 convert_element_type.3
  1.3 0.8 broadcast_in_dim.2.mod
  2.1 105.8 %shard_map.59 = (bf16[128,2688]{1,0:T(8,128)(2,1)}, f32[1,1344,512]{2,1,0:T(8,128)}) custom-call(bf16[128,2688]{1,0:T(8,128)(2,1)} %tok.1, bf16[512,128]{1,0:T(8,128)(2,1)} %broadcast_in_dim.2.mod, bf16[1,5376,512]{2,1,0:T(8,128)(2,1)} %weight_hbm.1, bf16[1,512,128]{2,1,0:T(8,128)(2,1)} %cot.1), custom_call_target="tpu_custom_call" | custom-call | tf_op jit(solution)/shard_map/pallas_call | solution.py:560
  108.0 105.4 %shard_map.60 = (bf16[128,2688]{1,0:T(8,128)(2,1)}, f32[1,1344,512]{2,1,0:T(8,128)}) custom-call(bf16[128,2688]{1,0:T(8,128)(2,1)} %get-tuple-element.4.tok_from, f32[1,1344,512]{2,1,0:T(8,128)} %get-tuple-element.5.weight_from), custom_call_target="tpu_custom_call" | custom-call | tf_op jit(solution)/shard_map/pallas_call | solution.py:580

commit v4 on v3

--- a/solution.py
+++ b/solution.py
@@ -179,18 +179,18 @@
     load.start()
     pl.semaphore_wait(barrier, len(devs))
 
-    def tok_part(pool, source, h):
-        return tokbuf.at[pool, pl.ds(pl.multiple_of(source * rows + h * part, part), part)]
+    def tok_part(pool, slot, h):
+        return tokbuf.at[pool, pl.ds(slot * rows + h * part, part)]
 
     for e, h in ((1, 0), (2, 1), (1, 1), (2, 0)):
         send(
-            tok.at[pl.ds(h * part, part)], tok_part(p, k, h), "tok_ka", 2 * e + h, (p, b, near[e])
+            tok.at[pl.ds(h * part, part)], tok_part(p, e, h), "tok_ka", 2 * e + h, (p, b, near[e])
         )
     for h in range(2):
-        send(tok.at[pl.ds(h * part, part)], tok_part(p, k, h), "tok_fw", h, partner)
+        send(tok.at[pl.ds(h * part, part)], tok_part(p, 0, h), "tok_fw", h, partner)
     for d in range(1, n_pb):
         send(mod, modbuf.at[b], "mod", d, pb_dev(d))
-    tokbuf[p, ka_rows(k), :] = tok[...]
+    tokbuf[p, :rows, :] = tok[...]
     modbuf[b] = mod[...]
 
     for i in range(half // 128):
@@ -218,26 +218,32 @@
         return modbuf[index].astype(F32)[:, :1] == p.astype(F32)
 
     def hand_on(e, h, relay_to):
-        region = tok_part(p, near[e], h)
+        region = tok_part(p, e, h)
         arrived(region, "tok_ka", 2 * e + h)
         if relay_to is not None:
-            send(region, region, "tok_ka", 6 + h, (p, b, near[relay_to]))
+            send(region, tok_part(p, 3, h), "tok_ka", 6 + h, (p, b, near[relay_to]))
         send(region, region, "tok_fw", 2 * e + h, partner)
 
-    def project(e):
-        for h in range(2):
-            arrived(tok_part(other, near[e], h), "tok_fw", 2 * e + h)
-        at = ka_rows(near[e])
+    arrivals = {}
+
+    def project(e, count):
+        for slot in range(e, e + count):
+            for h in range(2):
+                arrived(tok_part(other, slot, h), "tok_fw", 2 * slot + h)
+        at = pl.ds(e * rows, count * rows)
         proj = jnp.dot(tokbuf[0, at, :], wbuf[:half], preferred_element_type=F32)
         proj += jnp.dot(tokbuf[1, at, :], wbuf[half:], preferred_element_type=F32)
         projloc[at, :] = proj.astype(BF16)
         send(projloc.at[at], projrecv.at[at], "pj", e, partner)
+        arrivals[e] = at
 
     def settle(e):
         at = ka_rows(near[e])
-        arrived(projrecv.at[at], "pj", e)
+        slot = pl.ds(e * rows, rows)
+        if e in arrivals:
+            arrived(projrecv.at[arrivals[e]], "pj", e)
         owned = modbuf[b, at, :].astype(F32)[:, :1] == p.astype(F32)
-        projected = jnp.where(owned, projloc[at, :].astype(F32), projrecv[at, :].astype(F32))
+        projected = jnp.where(owned, projloc[slot, :].astype(F32), projrecv[slot, :].astype(F32))
         qbuf[at, :] = jnp.where(p == 0, projected[:, :hd], projected[:, hd : 2 * hd]).astype(BF16)
         kvbuf[b, near[e]] = projected[:, kv_at:].astype(BF16).reshape(2, part, 2 * hd)
         region = kvbuf.at[b, near[e], p]
@@ -251,20 +257,19 @@
             send(region, region, "kv_fw", d * n_ka + e, partner)
 
     load.wait()
-    project(0)
+    project(0, 1)
     hand_on(1, 0, 2)
     hand_on(2, 1, 1)
     settle(0)
     hand_on(1, 1, None)
     hand_on(2, 0, None)
-    project(1)
-    project(2)
+    project(1, 2)
     settle(1)
     settle(2)
     pass_keys(0)
     hand_on(3, 0, None)
     hand_on(3, 1, None)
-    project(3)
+    project(3, 1)
 
     @pl.when(mine)
     def _():
@@ -344,13 +349,6 @@
     for d in range(1, n_pb):
         send(dq_own, dq_own, "dq_z", d, pb_dev(d))
 
-    @pl.when(mine)
-    def _():
-        for d in range(1, n_ka):
-            region = xtbuf.at[:, :, ka_rows(k_from(d))]
-            arrived(region, "xt_ka", d)
-            remote(region, region, "xt_fw", d, partner).start()
-
     total = dkvs[b].astype(F32)
     for d in range(1, n_pb):
         arrived(dkvr.at[d], "dk_z", d)
@@ -412,7 +410,16 @@
 
     lax.fori_loop(0, n_c, back_chunk, 0)
     pool_sum(n_c - 1)
-    relay_sums(0)
+    @pl.when(mine)
+    def _():
+        for d in range(1, n_ka):
+            region = xtbuf.at[:, :, ka_rows(k_from(d))]
+            arrived(region, "xt_ka", d)
+            remote(region, region, "xt_fw", d, partner).start()
+
+    early = min(3, n_c)
+    for c in range(early):
+        relay_sums(c)
 
     for d in range(1, n_pb):
         region = gp.at[b_from(d), :, q_cols(p)]
@@ -435,7 +442,7 @@
         for d in range(n_ka):
             arrived(xtbuf.at[:, :, ka_rows(k_from(d))], "xt_fw", d)
 
-    tiles = n_c - 1 if n_c > 1 and slice_rows % (16 * (n_c - 1)) == 0 else 1
+    tiles = max(t for t in range(1, 7) if slice_rows % (16 * t) == 0)
     w_tile = slice_rows // tiles
 
     def weight_rows(t):
@@ -446,17 +453,17 @@
         wout[at, :] = acc
 
     def weight_and_relay(t, carry):
-        relay_sums(t + 1)
-
-        @pl.when(t < tiles)
+        weight_rows(t)
+
+        @pl.when(t + early < n_c)
         def _():
-            weight_rows(t)
+            relay_sums(t + early)
 
         return carry
 
-    lax.fori_loop(0, n_c - 1, weight_and_relay, 0)
-    if n_c == 1:
-        weight_rows(0)
+    lax.fori_loop(0, tiles, weight_and_relay, 0)
+    for c in range(early + tiles, n_c):
+        relay_sums(c)
     store = pltpu.make_async_copy(wout, out_weight.at[0], store_sem)
     store.start()
 
@@ -498,23 +505,31 @@
     lax.fori_loop(0, n_c, sent, 0)
 
 
-def hand_over(tok_from, weight_from, tok_to, weight_to, sems):
-    count = sems.shape[0]
-    copies = []
-    for source, target, first, parts in (
-        (tok_from, tok_to, 0, 2),
-        (weight_from.at[0], weight_to.at[0], 2, count - 2),
+def hand_over(tok_from, weight_from, tok_to, weight_to, tok_mid, weight_mid, in_sems, out_sems):
+    count = in_sems.shape[0]
+    pieces = []
+    for source, middle, target, first, parts in (
+        (weight_from.at[0], weight_mid, weight_to.at[0], 0, count - 1),
+        (tok_from, tok_mid, tok_to, count - 1, 1),
     ):
-        if source.shape[0] % (8 * parts * 2):
+        if source.shape[0] % (16 * parts):
             parts = 1
         rows = source.shape[0] // parts
         for i in range(parts):
             at = pl.ds(i * rows, rows)
-            copies.append(pltpu.make_async_copy(source.at[at], target.at[at], sems.at[first + i]))
-    for copy in copies:
-        copy.start()
-    for copy in copies:
-        copy.wait()
+            pieces.append(
+                (
+                    pltpu.make_async_copy(source.at[at], middle.at[at], in_sems.at[first + i]),
+                    pltpu.make_async_copy(middle.at[at], target.at[at], out_sems.at[first + i]),
+                )
+            )
+    for read, _ in pieces:
+        read.start()
+    for read, write in pieces:
+        read.wait()
+        write.start()
+    for _, write in pieces:
+        write.wait()
 
 
 def shards(tokens, modality, proj_weight, out_grad):
@@ -582,7 +597,12 @@
         out_shape=tuple(jax.ShapeDtypeStruct(x.shape, x.dtype) for x in made),
         in_specs=[any_space, any_space],
         out_specs=(any_space, any_space),
-        scratch_shapes=[pltpu.SemaphoreType.DMA((8,))],
+        scratch_shapes=[
+            pltpu.VMEM(made[0].shape, made[0].dtype),
+            pltpu.VMEM(made[1].shape[1:], made[1].dtype),
+            pltpu.SemaphoreType.DMA((5,)),
+            pltpu.SemaphoreType.DMA((5,)),
+        ],
         compiler_params=pltpu.CompilerParams(vmem_limit_bytes=62 * 2**20),
     )(*made)
 

time: 217 us -> 109 us (0.50); the launches traced: 214 us -> 109 us
  Pallas kernels: 211 us -> 107 us
    pallas_call x1, Pallas kernels: 105 us -> 2.94 us  [shards(): pl.pallas_call(hand_over, out_shape=tuple((jax.ShapeDtypeStruct(x.shape,...]
where the time goes in v4:
time: 109 us
  Pallas kernels  107 us (98%)
    pallas_call x1, Pallas kernels, shards(): pl.pallas_call(functools.partial(fused, dims), out_shape=(jax.ShapeDtypeS...  104 us
    pallas_call x1, Pallas kernels, shards(): pl.pallas_call(hand_over, out_shape=tuple((jax.ShapeDtypeStruct(x.shape,...  2.94 us

profile of v4, /device:TPU:10, one launch (start us, length us, event | category | flops | bytes accessed | tf_op | source)
XLA Modules:
  0.0 108.9 jit_solution(13085052568726557665)
XLA Ops:
  0.6 0.7 convert_element_type.3
  1.3 0.8 broadcast_in_dim.2.mod
  2.1 103.9 %shard_map.59 = (bf16[128,2688]{1,0:T(8,128)(2,1)}, f32[1,1344,512]{2,1,0:T(8,128)}) custom-call(bf16[128,2688]{1,0:T(8,128)(2,1)} %tok.1, bf16[512,128]{1,0:T(8,128)(2,1)} %broadcast_in_dim.2.mod, bf16[1,5376,512]{2,1,0:T(8,128)(2,1)} %weight_hbm.1, bf16[1,512,128]{2,1,0:T(8,128)(2,1)} %cot.1), custom_call_target="tpu_custom_call" | custom-call | tf_op jit(solution)/shard_map/pallas_call | solution.py:575
  106.0 2.9 %shard_map.60 = (bf16[128,2688]{1,0:T(8,128)(2,1)}, f32[1,1344,512]{2,1,0:T(8,128)}) custom-call(bf16[128,2688]{1,0:T(8,128)(2,1)} %get-tuple-element.4.tok_from, f32[1,1344,512]{2,1,0:T(8,128)} %get-tuple-element.5.weight_from), custom_call_target="tpu_custom_call" | custom-call | tf_op jit(solution)/shard_map/pallas_call | solution.py:595

commit v5 on v4

--- a/solution.py
+++ b/solution.py
@@ -289,8 +289,6 @@
             arrived(kvbuf.at[b_from(d), near[e], other], "kv_fw", d * n_ka + e)
 
     keys = n_pb * q_rows
-    key_rows = kvbuf[:, :, :, :, :hd].reshape(keys, hd)
-    ktbuf[...] = jnp.transpose(key_rows.astype(F32)).astype(BF16)
     tile = min(256, q_rows)
     for t in range(q_rows // tile):
         at = slice(t * tile, (t + 1) * tile)
@@ -326,6 +324,8 @@
         key_block(d)
         if i:
             key_sum(turns[i - 1])
+    key_rows = kvbuf[:, :, :, :, :hd].reshape(keys, hd)
+    ktbuf[...] = jnp.transpose(key_rows.astype(F32)).astype(BF16)
     key_sum(0)
     dq = jnp.dot(ktbuf[...], score[...].reshape(keys, q_rows), preferred_element_type=F32) * scaling
     dq = jnp.transpose(dq).astype(BF16)

time: 109 us -> 109 us (level)
  no operation moved by 1% of the time
where the time goes in v5:
time: 109 us
  Pallas kernels  107 us (98%)
    pallas_call x1, Pallas kernels, shards(): pl.pallas_call(functools.partial(fused, dims), out_shape=(jax.ShapeDtypeS...  104 us
    pallas_call x1, Pallas kernels, shards(): pl.pallas_call(hand_over, out_shape=tuple((jax.ShapeDtypeStruct(x.shape,...  2.94 us

profile of v5, /device:TPU:10, one launch (start us, length us, event | category | flops | bytes accessed | tf_op | source)
XLA Modules:
  0.0 108.9 jit_solution(9644865034216589468)
XLA Ops:
  0.6 0.7 convert_element_type.3
  1.3 0.8 broadcast_in_dim.2.mod
  2.1 103.9 %shard_map.59 = (bf16[128,2688]{1,0:T(8,128)(2,1)}, f32[1,1344,512]{2,1,0:T(8,128)}) custom-call(bf16[128,2688]{1,0:T(8,128)(2,1)} %tok.1, bf16[512,128]{1,0:T(8,128)(2,1)} %broadcast_in_dim.2.mod, bf16[1,5376,512]{2,1,0:T(8,128)(2,1)} %weight_hbm.1, bf16[1,512,128]{2,1,0:T(8,128)(2,1)} %cot.1), custom_call_target="tpu_custom_call" | custom-call | tf_op jit(solution)/shard_map/pallas_call | solution.py:575
  106.0 2.9 %shard_map.60 = (bf16[128,2688]{1,0:T(8,128)(2,1)}, f32[1,1344,512]{2,1,0:T(8,128)}) custom-call(bf16[128,2688]{1,0:T(8,128)(2,1)} %get-tuple-element.4.tok_from, f32[1,1344,512]{2,1,0:T(8,128)} %get-tuple-element.5.weight_from), custom_call_target="tpu_custom_call" | custom-call | tf_op jit(solution)/shard_map/pallas_call | solution.py:595
